TPU v7x, 128 devices: a whole 4x4x4 slice. The times are simulated.
128 devices in a mesh: expert: 32 (over y_hi, z, x), width: 4 (over y_lo, core).
Axes of the slice: x: 4, y: 4 (y_hi: 2, y_lo: 2; y = y_hi * 2 + y_lo), z: 4, core: 2. Of those that a mesh axis runs over, the one named last changes fastest.
Arguments:
- tokens: bfloat16 [4096, 2880], P('expert', 'width'), may hold values from -6 to 6
- grad_out: bfloat16 [4096, 2880], P('expert', 'width'), may hold values from -6 to 6
- routes: int32 [4096, 4], P('expert'), may hold values from 0 to 127, all different within a row; in each aligned block of 128 rows (0 to 127, 128 to 255, ...) at most 5 rows name the same one
- gates: float32 [4096, 4], P('expert'), may hold values from 0.05 to 1
- ranks: int32 [128], P('expert'), may hold values from 64 to 512
- w_gate: bfloat16 [2880, 2880], P('expert', 'width'), may hold values from -0.109375 to 0.109375
- w_up: bfloat16 [2880, 2880], P('expert', 'width'), may hold values from -0.109375 to 0.109375
- w_down: bfloat16 [2880, 2880], P('width', 'expert'), may hold values from -0.109375 to 0.109375
- delta_in: bfloat16 [128, 2880, 512], P('expert', 'width'), may hold values from -0.109375 to 0.109375
- delta_out: bfloat16 [128, 512, 2, 2880], P('expert', None, None, 'width'), may hold values from -0.25 to 0.25
Outputs:
- grad_tokens: bfloat16 [4096, 2880], P('expert', 'width')
- grad_gate: bfloat16 [2880, 2880], P('expert', 'width')
- grad_up: bfloat16 [2880, 2880], P('expert', 'width')
- grad_down: bfloat16 [2880, 2880], P('width', 'expert')
- grad_delta_in: bfloat16 [128, 2880, 512], P('expert', 'width')
- grad_delta_out: bfloat16 [128, 512, 2, 2880], P('expert', None, None, 'width')
Inputs may be any that keep to these rules, and one draw needn't show every extreme that they name: `routes`: each row names 4 different experts; among the 128 rows of one index of the expert axis (aligned blocks) no expert is named by more than 5 rows, a bound that some block reaches in every draw.
All inputs are finite; a program needn't handle non-finite values.
Results may differ from a plain program's by a relative error of at most 0.03.
Values may be sent and summed in bfloat16 or wider, within the bound.
No kernel may reach another device: no remote copies, remote signals or barrier semaphores. Data moves between devices by JAX's collectives and lax.ppermute only.
A program may use at most 128 MiB of HBM per device.

v0:
```python
import jax
import jax.numpy as jnp
from jax import lax
from jax.sharding import PartitionSpec as P


def local(tokens, grad_out, routes, gates, ranks, w_gate, w_up, w_down, delta_in, delta_out):
    precise = lax.Precision.HIGHEST
    over_rows = (((0,), (0,)), ((), ()))
    over_cols = (((1,), (1,)), ((), ()))
    expert_count = lax.axis_size("expert")
    token_rows, part_width = tokens.shape
    top_count = routes.shape[1]
    local_experts = delta_in.shape[0]
    rank_max = delta_in.shape[2]
    hidden_part = w_gate.shape[1]
    experts = local_experts * expert_count
    capacity = max(2, 5 * token_rows * top_count // (4 * experts))
    slot_count = experts * capacity
    whole_x, whole_dy = (
        lax.all_gather(tokens, "width", axis=1, tiled=True),
        lax.all_gather(grad_out, "width", axis=1, tiled=True),
    )
    weight_both = jnp.concatenate([w_gate, w_up], axis=1)
    full_both = lax.all_gather(weight_both, "expert", axis=0, tiled=True)
    base_both = jnp.dot(whole_x, full_both, preferred_element_type=jnp.float32)
    base_both = base_both.astype(jnp.bfloat16)
    columns = whole_dy
    down_grad = lax.dot_general(
        columns,
        lax.all_gather(w_down, "expert", axis=1, tiled=True),
        over_cols,
        preferred_element_type=jnp.float32,
    )
    flat_routes = routes.reshape(-1)
    expert_ids = lax.broadcasted_iota(jnp.int32, (1, experts), 1)
    onehot = (flat_routes[:, None] == expert_ids).astype(jnp.int32)
    before = jnp.cumsum(onehot, axis=0) - onehot
    slot_index = jnp.sum(before * onehot, axis=1)
    target = flat_routes * capacity + slot_index
    slot_ids = lax.broadcasted_iota(jnp.int32, (slot_count, 1), 0)
    slot_map = (target[None, :] == slot_ids).astype(jnp.float32)
    weighted = (
        (slot_map * gates.reshape(1, -1)).reshape(slot_count, token_rows, top_count).sum(axis=2)
    )
    picker = slot_map.reshape(slot_count, token_rows, top_count).sum(axis=2).astype(jnp.bfloat16)
    moved_rows = jnp.dot(
        picker, jnp.concatenate([tokens, base_both], axis=1), preferred_element_type=jnp.float32
    ).astype(jnp.bfloat16)
    pair_down = jnp.dot(weighted, down_grad, precision=precise).astype(jnp.bfloat16)
    outgoing = jnp.concatenate([moved_rows, pair_down], axis=1).reshape(
        expert_count, local_experts, capacity, -1
    )
    incoming = lax.all_to_all(outgoing, "expert", split_axis=0, concat_axis=2, tiled=True)
    incoming = incoming.reshape(local_experts, expert_count * capacity, -1)
    rows_x = incoming[:, :, :part_width]
    base_in = incoming[:, :, part_width : part_width + 2 * hidden_part].astype(jnp.float32)
    base_in = base_in.reshape(local_experts, -1, 2, hidden_part)
    down_in = incoming[:, :, part_width + 2 * hidden_part :].astype(jnp.float32)
    rank_mask = (
        lax.broadcasted_iota(jnp.int32, (local_experts, 1, rank_max), 2) < ranks[:, None, None]
    ).astype(jnp.float32)
    partial_low = jnp.einsum("erd,edk->erk", rows_x, delta_in, preferred_element_type=jnp.float32)
    low_rank = (
        lax.psum(partial_low.astype(jnp.bfloat16), "width").astype(jnp.float32) * rank_mask
    ).astype(jnp.bfloat16)
    pre_act = base_in + jnp.einsum(
        "erk,ekcf->ercf", low_rank, delta_out, preferred_element_type=jnp.float32
    )
    activation = pre_act[:, :, 0]
    up_value = pre_act[:, :, 1]
    sigmoid_act = jax.nn.sigmoid(activation)
    swish_value = activation * sigmoid_act
    hidden = (swish_value * up_value).astype(jnp.bfloat16)
    grad_act = down_in * up_value * sigmoid_act * (1.0 + activation * (1.0 - sigmoid_act))
    grad_upper = down_in * swish_value
    pair_grad = jnp.stack([grad_act, grad_upper], axis=2).astype(jnp.bfloat16)
    grad_delta_out = jnp.einsum(
        "erk,ercf->ekcf", low_rank, pair_grad, preferred_element_type=jnp.float32
    ).astype(jnp.bfloat16)
    partial_back = jnp.einsum(
        "ercf,ekcf->erk", pair_grad, delta_out, preferred_element_type=jnp.float32
    )
    low_grad = (
        lax.psum(partial_back.astype(jnp.bfloat16), "width").astype(jnp.float32) * rank_mask
    ).astype(jnp.bfloat16)
    grad_delta_in = jnp.einsum(
        "erd,erk->edk", rows_x, low_grad, preferred_element_type=jnp.float32
    ).astype(jnp.bfloat16)
    back_rows = jnp.einsum(
        "erk,edk->erd", low_grad, delta_in, preferred_element_type=jnp.float32
    ).astype(jnp.bfloat16)
    returning = jnp.concatenate(
        [back_rows, hidden, pair_grad.reshape(local_experts, -1, 2 * hidden_part)], axis=2
    )
    returning = returning.reshape(local_experts, expert_count, capacity, -1)
    arrived = lax.all_to_all(returning, "expert", split_axis=1, concat_axis=0, tiled=True).reshape(
        slot_count, -1
    )
    back_in = arrived[:, :part_width]
    hidden_back = arrived[:, part_width : part_width + hidden_part].astype(jnp.float32)
    grads_back = arrived[:, part_width + hidden_part :]
    token_back = lax.dot_general(picker, back_in, over_rows, preferred_element_type=jnp.float32)
    mixed_hidden = lax.dot_general(weighted, hidden_back, over_rows, precision=precise).astype(
        jnp.bfloat16
    )
    summed = lax.dot_general(
        picker, grads_back, over_rows, preferred_element_type=jnp.float32
    ).astype(jnp.bfloat16)
    columns = whole_x
    base_share = lax.psum_scatter(
        lax.dot_general(columns, summed, over_rows, preferred_element_type=jnp.float32).astype(
            jnp.bfloat16
        ),
        "expert",
        scatter_dimension=0,
        tiled=True,
    ).astype(jnp.float32)
    columns = whole_dy
    down_share = lax.psum_scatter(
        lax.dot_general(
            columns, mixed_hidden, over_rows, preferred_element_type=jnp.float32
        ).astype(jnp.bfloat16),
        "expert",
        scatter_dimension=0,
        tiled=True,
    ).astype(jnp.float32)
    grad_gate = base_share[:, :hidden_part].astype(jnp.bfloat16)
    grad_up = base_share[:, hidden_part:].astype(jnp.bfloat16)
    grad_down = down_share.T.astype(jnp.bfloat16)
    partial_tokens = lax.dot_general(
        summed, full_both, over_cols, preferred_element_type=jnp.float32
    )
    token_grad = lax.psum_scatter(
        partial_tokens.astype(jnp.bfloat16), "width", scatter_dimension=1, tiled=True
    ).astype(jnp.float32)
    grad_tokens = (token_grad + token_back).astype(jnp.bfloat16)
    return (grad_tokens, grad_gate, grad_up, grad_down, grad_delta_in, grad_delta_out)


def solution(mesh):
    return jax.shard_map(
        local,
        mesh=mesh,
        in_specs=(
            P("expert", "width"),
            P("expert", "width"),
            P("expert", None),
            P("expert", None),
            P("expert"),
            P("expert", "width"),
            P("expert", "width"),
            P("width", "expert"),
            P("expert", "width", None),
            P("expert", None, None, "width"),
        ),
        out_specs=(
            P("expert", "width"),
            P("expert", "width"),
            P("expert", "width"),
            P("width", "expert"),
            P("expert", "width", None),
            P("expert", None, None, "width"),
        ),
        check_vma=False,
    )
```

profile of v0, /device:TPU:0, one launch (start us, length us, event | category | flops | bytes accessed | tf_op | source)
XLA Modules:
  0.0 932.4 jit_solution(17404453836838803674)
XLA Ops:
  12.1 10.1 %all_gather.14 = bf16[128,2880]{0,1:T(8,128)(2,1)} all-gather(bf16[128,720]{0,1:T(8,128)(2,1)} %param.11), channel_id=1, replica_groups=mesh['expert'=32,'width'=4] {'width'}, dimensions={1}, use_global_device_ids=true | all-gather | bytes 921600 | tf_op jit(solution)/shard_map/all_gather | solution.py:22
  22.2 10.1 %all_gather.13 = bf16[128,2880]{0,1:T(8,128)(2,1)} all-gather(bf16[128,720]{0,1:T(8,128)(2,1)} %param.10), channel_id=1, replica_groups=mesh['expert'=32,'width'=4] {'width'}, dimensions={1}, use_global_device_ids=true | all-gather | bytes 921600 | tf_op jit(solution)/shard_map/all_gather | solution.py:21
  32.4 65.0 %all-gather.7.cloned.1.call-done = bf16[32,90,720]{2,1,0:T(8,128)(2,1)} async-done(((bf16[1,90,720]{2,1,0:T(8,128)(2,1)}), bf16[32,90,720]{2,1,0:T(8,128)(2,1)}) %all-gather.7.cloned.1.call-update) | async-done | bytes 4147216 | tf_op jit(solution)/shard_map/all_gather | solution.py:31
  97.4 7.5 reshape.121
  104.9 4.3 fusion.47
  111.7 96.8 %all-gather.5.cloned.1.call-done = bf16[32,90,1440]{2,1,0:T(8,128)(2,1)} async-done(((bf16[1,90,1440]{2,1,0:T(8,128)(2,1)}), bf16[32,90,1440]{2,1,0:T(8,128)(2,1)}) %all-gather.5.cloned.1.call-update) | async-done | bytes 8294416 | tf_op jit(solution)/shard_map/all_gather | solution.py:25
  208.5 11.0 %reshape.119 = bf16[2880,1440]{1,0:T(8,128)(2,1)} reshape(bf16[32,90,1440]{2,1,0:T(8,128)(2,1)} %all-gather.5.cloned.1.call-done) | data formatting | bytes 16588800
  219.6 6.2 fusion.4
  229.1 6.2 copy.125
  235.3 7.3 reshape.111
  246.9 52.6 %all_to_all.30 = bf16[32,4,5,2880]{3,1,2,0:T(4,128)(2,1)S(1)} all-to-all(bf16[32,4,5,2880]{3,1,2,0:T(4,128)(2,1)S(1)} %copy.126), channel_id=1, replica_groups=mesh['expert'=32,'width'=4] {'expert'}, dimensions={0} | all-to-all | bytes 7372800 | tf_op jit(solution)/shard_map/all_to_all | solution.py:54
  312.9 6.5 reshape.117
  319.4 22.2 %all-reduce.7.cloned.1.call-done = bf16[4,160,512]{2,1,0:T(8,128)(2,1)} async-done(((bf16[4,160,512]{2,1,0:T(8,128)(2,1)}), bf16[4,160,512]{2,1,0:T(8,128)(2,1)}) %all-reduce.7.cloned.1.call-update) | async-done | bytes 655376 | tf_op jit(solution)/shard_map/psum | solution.py:65
  341.6 6.1 copy_add_fusion
  367.8 6.2 convert_element_type.132
  378.1 18.8 %all-reduce.9.cloned.1.call-done = bf16[4,160,512]{2,1,0:T(8,128)(2,1)} async-done(((bf16[4,160,512]{2,1,0:T(8,128)(2,1)}), bf16[4,160,512]{2,1,0:T(8,128)(2,1)}) %all-reduce.9.cloned.1.call-update) | async-done | bytes 655376 | tf_op jit(solution)/shard_map/psum | solution.py:85
  400.7 13.1 %concatenate.19 = bf16[4,32,5,2880]{3,0,2,1:T(4,128)(2,1)} concatenate(bf16[4,32,5,720]{3,0,2,1:T(4,128)(2,1)} %bitcast.111, bf16[4,32,5,720]{3,0,2,1:T(4,128)(2,1)} %fusion.16, bf16[4,32,5,1440]{3,0,2,1:T(4,128)(2,1)} %convert_element_type.132), dimensions={3} | concatenate | bytes 7372800 | tf_op jit(solution)/shard_map/concatenate | solution.py:93
  413.8 57.8 %all_to_all.31 = bf16[4,32,5,2880]{3,0,2,1:T(4,128)(2,1)S(1)} all-to-all(bf16[4,32,5,2880]{3,0,2,1:T(4,128)(2,1)} %concatenate.19), channel_id=1, replica_groups=mesh['expert'=32,'width'=4] {'expert'}, dimensions={1} | all-to-all | bytes 7372800 | tf_op jit(solution)/shard_map/all_to_all | solution.py:97
  475.0 8.0 reshape.115
  487.0 6.9 convolution_convert_fusion.3
  497.0 4.5 fusion.3
  501.5 5.6 fusion
  509.0 6.1 convolution_convert_fusion.4
  520.2 400.1 %all-reduce.11.cloned.1.call-done = (bf16[2880,1440]{0,1:T(8,128)(2,1)}, bf16[2880,720]{0,1:T(8,128)(2,1)}) async-done(((bf16[2880,1440]{0,1:T(8,128)(2,1)}, bf16[2880,720]{0,1:T(8,128)(2,1)}), (bf16[2880,1440]{0,1:T(8,128)(2,1)}, bf16[2880,720]{0,1:T(8,128)(2,1)})) %all-reduce.11.cloned.1.call-update) | async-done | bytes 12441616
  (103 shorter events, 77.9 us)
Async XLA Ops:
  7.2 297.4 %copy-start = (bf16[4,720,512]{2,1,0:T(8,128)(2,1)S(1)}, bf16[4,720,512]{2,1,0:T(8,128)(2,1)}, u32[]{:S(2)}) copy-start(bf16[4,720,512]{2,1,0:T(8,128)(2,1)} %param.18) | copy-start | bytes 8847364
  7.2 4.6 copy-start.15
  7.2 4.6 copy-start.16
  7.2 90.2 %all-gather.7.cloned.1.call-start = ((), (), s32[]{:S(2)}) async-start(), calls=%async_computation.7 | async-start | bytes 4866048 | tf_op jit(solution)/shard_map/all_gather | solution.py:31
  7.9 200.6 %all-gather.5.cloned.1.call-start = ((), (), s32[]{:S(2)}) async-start(), calls=%async_computation.6 | async-start | bytes 9732096 | tf_op jit(solution)/shard_map/all_gather | solution.py:25
  9.9 331.7 %all-reduce.7.cloned.1.call-start = ((), (), s32[]{:S(2)}) async-start(), calls=%async_computation.3 | async-start | bytes 1310720 | tf_op jit(solution)/shard_map/psum | solution.py:65
  219.6 6.3 copy-start.14
  225.8 1.2 copy-start.9
  299.4 1.9 copy-start.1
  303.6 1.0 copy-start.4
  303.6 2.6 copy-start.17
  306.2 90.7 %all-reduce.9.cloned.1.call-start = ((), (), s32[]{:S(2)}) async-start(), calls=%async_computation.4 | async-start | bytes 1310720 | tf_op jit(solution)/shard_map/psum | solution.py:85
  341.6 10.8 %slice-start = ((s8[5898240]{0:T(1024)(128)(4,1)}), s8[4194304]{0:T(1024)(128)(4,1)S(1)}, s32[]{:S(2)}) async-start(s8[5898240]{0:T(1024)(128)(4,1)} %bitcast.109), calls=%async_computation.9 | async-start | bytes 8388608
  347.7 2.2 copy-start.8
  347.7 4.7 slice-start.1
  351.1 1.2 copy-start.7
  357.4 160.3 %reduce-scatter.4.cloned.1.call-start = ((), (), s32[]{:S(2)}) async-start(), calls=%async_computation.5 | async-start | bytes 921600 | tf_op jit(solution)/shard_map/reduce_scatter | solution.py:134
  357.7 4.3 copy-start.3
  361.9 2.5 copy-start.2
  493.9 426.3 %all-reduce.11.cloned.1.call-start = ((), (), s32[]{:S(2)}) async-start(), calls=%async_computation.8 | async-start | bytes 25436160
  496.9 4.5 copy-start.10
  496.9 4.5 copy-start.13
  509.0 6.2 copy-start.5
  509.0 6.2 copy-start.11
  (3 other events, 2.4 us)
Sparse Core Ops, SparseCore 0:
  11.1 86.2 all-gather.6
  100.5 108.0 all-gather.4
  306.3 35.2 all-reduce.6
  357.5 39.2 all-reduce.8
  494.1 14.8 reduce-scatter.3
  511.4 408.7 all-reduce.10
where the time goes:
time: 943 us; the launch traced here: 932 us
  waiting for transfers between devices  604 us (64%)
  blocking collectives  131 us (14%)
  local copies, waits for them, and re-layouts  106 us (11%)
  matrix products  60.4 us (6%)
  other arithmetic  15.6 us (2%)
  between operations  15.5 us (2%)
    unnamed x7, waiting for transfers between devices  401 us
    all_gather x1, waiting for transfers between devices, local(): full_both = lax.all_gather(weight_both, 'expert', axis=0, tiled=True)  96.8 us
    all_gather x1, waiting for transfers between devices, local(): lax.all_gather(w_down, 'expert', axis=1, tiled=True)  65 us
    all_to_all x1, blocking collectives, local(): lax.all_to_all(returning, 'expert', split_axis=1, concat_axis=0, tiled=True)  57.8 us
    all_to_all x1, blocking collectives, local(): lax.all_to_all(outgoing, 'expert', split_axis=0, concat_axis=2, tiled=True)  52.6 us
    unnamed x50, local copies, waits for them, and re-layouts  28.1 us
    psum x1, waiting for transfers between devices, local(): lax.psum(partial_low.astype(jnp.bfloat16), 'width').astype(jnp.float32)  22.2 us
  transfers between devices with their start and end apart: 6, of which 5 were waited for; matrix products, arithmetic and copies ran while one was open for 8% of the time, Pallas kernels for 0%

commit v1 on v0

--- a/solution.py
+++ b/solution.py
@@ -22,7 +22,9 @@
         lax.all_gather(grad_out, "width", axis=1, tiled=True),
     )
     weight_both = jnp.concatenate([w_gate, w_up], axis=1)
-    full_both = lax.all_gather(weight_both, "expert", axis=0, tiled=True)
+    full_both = jnp.concatenate(
+        lax.all_to_all(jnp.stack([weight_both] * lax.axis_size("expert")), "expert", 0, 0), axis=0
+    )
     base_both = jnp.dot(whole_x, full_both, preferred_element_type=jnp.float32)
     base_both = base_both.astype(jnp.bfloat16)
     columns = whole_dy

time: 943 us -> 954 us (1.012)
  blocking collectives: 131 us -> 256 us
  waiting for transfers between devices: 604 us -> 481 us
  starting transfers between devices: 0.46 us -> 11.5 us
    all_gather x1, blocking collectives: 10.1 us -> 135 us  [local(): lax.all_gather(grad_out, 'width', axis=1, tiled=True)]
    all_gather x1 -> x0, waiting for transfers between devices: 96.8 us -> none  [local(): full_both = lax.all_gather(weight_both, 'expert', axis=0, tiled=True)]
    all_gather x1, waiting for transfers between devices: 65 us -> 38.1 us  [local(): lax.all_gather(w_down, 'expert', axis=1, tiled=True)]
    unnamed x50 -> x49, local copies, waits for them, and re-layouts: 28.1 us -> 16.3 us
    all_to_all x0 -> x1, starting transfers between devices: none -> 11.1 us  [local(): lax.all_to_all(jnp.stack([weight_both] * lax.axis_size('expert')), 'exper...]
    reshape x0 -> x1, local copies, waits for them, and re-layouts: none -> 11.1 us  [local(): jnp.concatenate(lax.all_to_all(jnp.stack([weight_both] * lax.axis_size('e...]
    unnamed x7 -> x6, waiting for transfers between devices: 401 us -> 402 us
  transfers between devices with their start and end apart: 6 -> 6, of which waited for: 5 -> 4; matrix products, arithmetic and copies ran while one was open for 8% -> 8% of each run, Pallas kernels for 0% -> 0%
where the time goes in v1:
time: 954 us; the launch traced here: 949 us
  waiting for transfers between devices  481 us (50%)
  blocking collectives  256 us (27%)
  local copies, waits for them, and re-layouts  110 us (12%)
  matrix products  60.4 us (6%)
  between operations  15.1 us (2%)
  other arithmetic  14.9 us (2%)
  starting transfers between devices  11.5 us (1%)
    unnamed x6, waiting for transfers between devices  402 us
    all_gather x1, blocking collectives, local(): lax.all_gather(grad_out, 'width', axis=1, tiled=True)  135 us
    all_to_all x1, blocking collectives, local(): lax.all_to_all(returning, 'expert', split_axis=1, concat_axis=0, tiled=True)  57.8 us
    all_to_all x1, blocking collectives, local(): lax.all_to_all(outgoing, 'expert', split_axis=0, concat_axis=2, tiled=True)  52.6 us
    all_gather x1, waiting for transfers between devices, local(): lax.all_gather(w_down, 'expert', axis=1, tiled=True)  38.1 us
    psum x1, waiting for transfers between devices, local(): lax.psum(partial_low.astype(jnp.bfloat16), 'width').astype(jnp.float32)  22.1 us
  transfers between devices with their start and end apart: 6, of which 4 were waited for; matrix products, arithmetic and copies ran while one was open for 8% of the time, Pallas kernels for 0%

profile of v1, /device:TPU:0, one launch (start us, length us, event | category | flops | bytes accessed | tf_op | source)
XLA Modules:
  0.0 949.4 jit_solution(9392568349331959750)
XLA Ops:
  9.2 4.7 stack.8
  13.9 11.1 %all-to-all-start = ((bf16[32,90,1440]{2,1,0:T(8,128)(2,1)}), bf16[32,90,1440]{2,1,0:T(8,128)(2,1)}, u32[]{:S(2)}, u32[]{:S(2)}) async-start(bf16[32,90,1440]{2,1,0:T(8,128)(2,1)} %stack.8), calls=%async_computation | async-start | bytes 18874368 | tf_op jit(solution)/shard_map/all_to_all | solution.py:26
  26.6 134.8 %all_gather.10 = bf16[128,2880]{0,1:T(8,128)(2,1)} all-gather(bf16[128,720]{0,1:T(8,128)(2,1)} %param.11), channel_id=1, replica_groups=mesh['expert'=32,'width'=4] {'width'}, dimensions={1}, use_global_device_ids=true | all-gather | bytes 921600 | tf_op jit(solution)/shard_map/all_gather | solution.py:22
  161.4 11.0 %all_gather.9 = bf16[128,2880]{0,1:T(8,128)(2,1)} all-gather(bf16[128,720]{0,1:T(8,128)(2,1)} %param.10), channel_id=1, replica_groups=mesh['expert'=32,'width'=4] {'width'}, dimensions={1}, use_global_device_ids=true | all-gather | bytes 921600 | tf_op jit(solution)/shard_map/all_gather | solution.py:21
  172.4 38.1 %all-gather.3.cloned.1.call-done = bf16[32,90,720]{2,1,0:T(8,128)(2,1)} async-done(((bf16[1,90,720]{2,1,0:T(8,128)(2,1)}), bf16[32,90,720]{2,1,0:T(8,128)(2,1)}) %all-gather.3.cloned.1.call-update) | async-done | bytes 4147216 | tf_op jit(solution)/shard_map/all_gather | solution.py:33
  210.4 7.5 reshape.125
  224.8 11.1 %reshape.116 = bf16[2880,1440]{1,0:T(8,128)(2,1)} reshape(bf16[32,90,1440]{2,1,0:T(8,128)(2,1)} %all-to-all-done) | data formatting | bytes 16588800 | tf_op jit(solution)/shard_map/reshape | solution.py:25
  235.9 6.2 fusion.4
  245.4 6.2 copy.125
  251.5 7.4 reshape.117
  263.2 52.6 %all_to_all.35 = bf16[32,4,5,2880]{3,1,2,0:T(4,128)(2,1)S(1)} all-to-all(bf16[32,4,5,2880]{3,1,2,0:T(4,128)(2,1)S(1)} %copy.126), channel_id=1, replica_groups=mesh['expert'=32,'width'=4] {'expert'}, dimensions={0} | all-to-all | bytes 7372800 | tf_op jit(solution)/shard_map/all_to_all | solution.py:56
  329.1 6.5 reshape.123
  335.6 22.1 %all-reduce.7.cloned.1.call-done = bf16[4,160,512]{2,1,0:T(8,128)(2,1)} async-done(((bf16[4,160,512]{2,1,0:T(8,128)(2,1)}), bf16[4,160,512]{2,1,0:T(8,128)(2,1)}) %all-reduce.7.cloned.1.call-update) | async-done | bytes 655376 | tf_op jit(solution)/shard_map/psum | solution.py:67
  357.7 6.1 copy_add_fusion
  383.9 6.2 convert_element_type.132
  394.3 18.8 %all-reduce.9.cloned.1.call-done = bf16[4,160,512]{2,1,0:T(8,128)(2,1)} async-done(((bf16[4,160,512]{2,1,0:T(8,128)(2,1)}), bf16[4,160,512]{2,1,0:T(8,128)(2,1)}) %all-reduce.9.cloned.1.call-update) | async-done | bytes 655376 | tf_op jit(solution)/shard_map/psum | solution.py:87
  416.9 13.1 %concatenate.19 = bf16[4,32,5,2880]{3,0,2,1:T(4,128)(2,1)} concatenate(bf16[4,32,5,720]{3,0,2,1:T(4,128)(2,1)} %bitcast.109, bf16[4,32,5,720]{3,0,2,1:T(4,128)(2,1)} %fusion.16, bf16[4,32,5,1440]{3,0,2,1:T(4,128)(2,1)} %convert_element_type.132), dimensions={3} | concatenate | bytes 7372800 | tf_op jit(solution)/shard_map/concatenate | solution.py:95
  430.0 57.8 %all_to_all.36 = bf16[4,32,5,2880]{3,0,2,1:T(4,128)(2,1)S(1)} all-to-all(bf16[4,32,5,2880]{3,0,2,1:T(4,128)(2,1)} %concatenate.19), channel_id=1, replica_groups=mesh['expert'=32,'width'=4] {'expert'}, dimensions={1} | all-to-all | bytes 7372800 | tf_op jit(solution)/shard_map/all_to_all | solution.py:99
  491.3 8.0 reshape.121
  503.3 6.9 convolution_convert_fusion.3
  513.2 4.5 fusion.3
  517.7 5.6 fusion
  525.2 6.1 convolution_convert_fusion.4
  536.4 401.1 %all-reduce.11.cloned.1.call-done = (bf16[2880,1440]{0,1:T(8,128)(2,1)}, bf16[2880,720]{0,1:T(8,128)(2,1)}) async-done(((bf16[2880,1440]{0,1:T(8,128)(2,1)}, bf16[2880,720]{0,1:T(8,128)(2,1)}), (bf16[2880,1440]{0,1:T(8,128)(2,1)}, bf16[2880,720]{0,1:T(8,128)(2,1)})) %all-reduce.11.cloned.1.call-update) | async-done | bytes 12441616
  (103 shorter events, 80.9 us)
Async XLA Ops:
  7.2 313.7 %copy-start = (bf16[4,720,512]{2,1,0:T(8,128)(2,1)S(1)}, bf16[4,720,512]{2,1,0:T(8,128)(2,1)}, u32[]{:S(2)}) copy-start(bf16[4,720,512]{2,1,0:T(8,128)(2,1)} %param.18) | copy-start | bytes 8847364
  7.2 203.3 %all-gather.3.cloned.1.call-start = ((), (), s32[]{:S(2)}) async-start(), calls=%async_computation.7 | async-start | bytes 4866048 | tf_op jit(solution)/shard_map/all_gather | solution.py:33
  13.9 11.2 %copy-start.15 = (s32[128,4]{0,1:T(4,128)S(1)}, s32[128,4]{0,1:T(4,128)}, u32[]{:S(2)}) copy-start(s32[128,4]{0,1:T(4,128)} %param.12) | copy-start | bytes 6148
  13.9 12.4 %copy-start.16 = (f32[128,4]{0,1:T(4,128)S(1)}, f32[128,4]{0,1:T(4,128)}, u32[]{:S(2)}) copy-start(f32[128,4]{0,1:T(4,128)} %param.13) | copy-start | bytes 6148
  13.9 210.9 %all-to-all-start = ((bf16[32,90,1440]{2,1,0:T(8,128)(2,1)}), bf16[32,90,1440]{2,1,0:T(8,128)(2,1)}, u32[]{:S(2)}, u32[]{:S(2)}) async-start(bf16[32,90,1440]{2,1,0:T(8,128)(2,1)} %stack.8), calls=%async_computation | async-start | bytes 18874368 | tf_op jit(solution)/shard_map/all_to_all | solution.py:26
  25.0 332.7 %all-reduce.7.cloned.1.call-start = ((), (), s32[]{:S(2)}) async-start(), calls=%async_computation.4 | async-start | bytes 1310720 | tf_op jit(solution)/shard_map/psum | solution.py:67
  235.9 6.3 copy-start.14
  242.1 1.2 copy-start.9
  315.7 1.9 copy-start.1
  319.9 1.0 copy-start.4
  319.9 2.6 copy-start.17
  322.4 90.7 %all-reduce.9.cloned.1.call-start = ((), (), s32[]{:S(2)}) async-start(), calls=%async_computation.5 | async-start | bytes 1310720 | tf_op jit(solution)/shard_map/psum | solution.py:87
  357.7 10.8 %slice-start = ((s8[5898240]{0:T(1024)(128)(4,1)}), s8[4194304]{0:T(1024)(128)(4,1)S(1)}, s32[]{:S(2)}) async-start(s8[5898240]{0:T(1024)(128)(4,1)} %bitcast.107), calls=%async_computation.9 | async-start | bytes 8388608
  363.8 2.2 copy-start.8
  363.9 4.7 slice-start.1
  367.3 1.3 copy-start.7
  373.6 160.4 %reduce-scatter.4.cloned.1.call-start = ((), (), s32[]{:S(2)}) async-start(), calls=%async_computation.6 | async-start | bytes 921600 | tf_op jit(solution)/shard_map/reduce_scatter | solution.py:136
  373.8 4.3 copy-start.3
  378.1 2.5 copy-start.2
  510.2 427.3 %all-reduce.11.cloned.1.call-start = ((), (), s32[]{:S(2)}) async-start(), calls=%async_computation.8 | async-start | bytes 25436160
  513.2 4.5 copy-start.10
  513.2 4.5 copy-start.13
  525.2 6.2 copy-start.5
  525.2 6.2 copy-start.11
  (3 other events, 2.4 us)
Sparse Core Ops, SparseCore 0:
  11.1 199.3 all-gather.2
  322.5 35.1 all-reduce.6
  373.7 39.3 all-reduce.8
  510.3 14.8 reduce-scatter.3
  527.6 409.8 all-reduce.10
